TPU v7x, 32 devices: a whole 2x2x4 slice. The times are simulated.
32 devices in a mesh: ctx: 8 (over y, x, core), tp: 4 (over z).
Axes of the slice: x: 2, y: 2, z: 4, core: 2. Of those that a mesh axis runs over, the one named last changes fastest.
Arguments:
- gate: bfloat16 [3072, 8192], P('ctx', 'tp'), may hold values from -6 to 6
- key: bfloat16 [3072, 8192], P('ctx', 'tp'), may hold values from -6 to 6
- value: bfloat16 [3072, 8192], P('ctx', 'tp'), may hold values from -6 to 6
- filters: bfloat16 [128, 512], P(None, 'tp'), may hold values from -0.5 to 0.5
- lengths: int32 [16], replicated, may hold values from 1 to 1536, 3072 in all
- cotangent: bfloat16 [3072, 8192], P('ctx', 'tp'), may hold values from -6 to 6
Outputs:
- gate_grad: bfloat16 [3072, 8192], P('ctx', 'tp')
- key_grad: bfloat16 [3072, 8192], P('ctx', 'tp')
- value_grad: bfloat16 [3072, 8192], P('ctx', 'tp')
- filter_grad: float32 [128, 512], P('ctx', 'tp')
All inputs are finite; a program needn't handle non-finite values.
Results may differ from a plain program's by a relative error of at most 0.0049.
Values may be sent and summed in bfloat16 or wider, within the bound.
A program may use at most 128 MiB of HBM per device.

v0:
```python
import math

import jax
import jax.numpy as jnp
from jax import lax
from jax.sharding import PartitionSpec as P


def passed_along(value, axis, steps):
    count = lax.axis_size(axis)
    first, last = (max(0, -steps), min(count, count - steps))
    return lax.ppermute(value, axis, [(source, source + steps) for source in range(first, last)])


def band_table(tap_cols):
    tap_count, group_count = tap_cols.shape
    flipped = jnp.flip(tap_cols.T, axis=1)
    padded = jnp.concatenate(
        [
            jnp.zeros((group_count, 1), tap_cols.dtype),
            flipped,
            jnp.zeros((group_count, tap_count), tap_cols.dtype),
        ],
        axis=1,
    )
    tiled_rows = jnp.broadcast_to(padded[:, None, :], (group_count, tap_count, 2 * tap_count + 1))
    flat_rows = tiled_rows.reshape(group_count, tap_count * (2 * tap_count + 1))
    return flat_rows[:, : 2 * tap_count * tap_count].reshape(group_count, tap_count, 2 * tap_count)


def block_mask(lengths, first_row, tap_count):
    doc_ends = jnp.cumsum(lengths)
    row_ids = first_row + jnp.arange(tap_count, dtype=jnp.int32)
    doc_starts = jnp.sum(
        jnp.where(doc_ends[None, :] <= row_ids[:, None], lengths[None, :], 0), axis=1
    )
    col_ids = first_row - tap_count + jnp.arange(2 * tap_count, dtype=jnp.int32)
    return col_ids[None, :] >= doc_starts[:, None]


def on_device(gate, key, value, filters, lengths, cotangent):
    row_count, local_width = gate.shape
    tap_count, filt_count = filters.shape
    chan_group = local_width // filt_count
    block_count = row_count // tap_count
    ctx_count = lax.axis_size("ctx")
    row_base = lax.axis_index("ctx") * row_count
    grad_scale = 1.0 / math.sqrt(row_count * ctx_count)
    key_float = key.astype(jnp.float32)
    value_float = value.astype(jnp.float32)
    product = (key_float * value_float).astype(jnp.bfloat16)
    prior_tail = passed_along(product[row_count - tap_count :], "ctx", 1)
    extended = jnp.concatenate([prior_tail, product], axis=0)
    windows = jnp.concatenate(
        [
            extended[:row_count].reshape(block_count, tap_count, local_width),
            extended[tap_count:].reshape(block_count, tap_count, local_width),
        ],
        axis=1,
    )
    windows = windows.reshape(block_count, 2 * tap_count, filt_count, chan_group)
    filt_float = filters.astype(jnp.float32)
    band_tab = band_table(filt_float).astype(jnp.bfloat16)

    def banded_at(block_index):
        doc_mask = block_mask(lengths, row_base + block_index * tap_count, tap_count)
        return jnp.where(doc_mask[None], band_tab, jnp.zeros((), jnp.bfloat16))

    def forward_block(operands):
        block_index, window = operands
        return jnp.einsum(
            "fab,bfc->afc", banded_at(block_index), window, preferred_element_type=jnp.float32
        )

    block_ids = jnp.arange(block_count, dtype=jnp.int32)
    filtered = lax.map(forward_block, (block_ids, windows)).reshape(row_count, local_width)
    cot_float = cotangent.astype(jnp.float32)
    filt_cot = (cot_float * gate.astype(jnp.float32)).astype(jnp.bfloat16)
    gate_grad = (cot_float * filtered).astype(jnp.bfloat16)
    cot_blocks = filt_cot.reshape(block_count, tap_count, filt_count, chan_group)

    def backward_block(operands):
        block_index, cot_block = operands
        return jnp.einsum(
            "fab,afc->bfc", banded_at(block_index), cot_block, preferred_element_type=jnp.float32
        )

    spread = lax.map(backward_block, (block_ids, cot_blocks))
    returned = passed_along(spread[0, :tap_count], "ctx", -1)
    later_part = jnp.concatenate([spread[1:, :tap_count], returned[None]], axis=0)
    prod_grad = (spread[:, tap_count:] + later_part).reshape(row_count, local_width)
    key_grad = (prod_grad * value_float).astype(jnp.bfloat16)
    value_grad = (prod_grad * key_float).astype(jnp.bfloat16)

    def corr_step(running, operands):
        block_index, cot_block, window = operands
        doc_mask = block_mask(lengths, row_base + block_index * tap_count, tap_count)
        correl = jnp.einsum("afc,bfc->fab", cot_block, window, preferred_element_type=jnp.float32)
        return (running + jnp.where(doc_mask[None], correl, 0.0), None)

    corr_sum, unused = lax.scan(
        corr_step,
        jnp.zeros((filt_count, tap_count, 2 * tap_count), jnp.float32),
        (block_ids, cot_blocks, windows),
    )
    filt_local = jax.vjp(band_table, filt_float)[1](corr_sum)[0] * grad_scale
    share_rows = tap_count // ctx_count
    summed = lax.psum(filt_local, "ctx")
    filter_grad = lax.dynamic_slice_in_dim(
        summed, lax.axis_index("ctx") * share_rows, share_rows, 0
    )
    return (gate_grad, key_grad, value_grad, filter_grad)


def solution(mesh):
    return jax.shard_map(
        on_device,
        mesh=mesh,
        in_specs=(
            P("ctx", "tp"),
            P("ctx", "tp"),
            P("ctx", "tp"),
            P(None, "tp"),
            P(),
            P("ctx", "tp"),
        ),
        out_specs=(P("ctx", "tp"), P("ctx", "tp"), P("ctx", "tp"), P("ctx", "tp")),
        check_vma=False,
    )
```

profile of v0, /device:TPU:0, one launch (start us, length us, event | category | flops | bytes accessed | tf_op | source)
XLA Modules:
  0.0 395.8 jit_solution(267769961166762453)
XLA Ops:
  18.5 4.5 %broadcast_in_dim.164 = bf16[128,128,257]{0,2,1:T(8,128)(2,1)} broadcast(bf16[128,257]{0,1:T(8,128)(2,1)S(1)} %maximum_convert_fusion), dimensions={0,2} | broadcast | bytes 8487168 | tf_op jit(solution)/shard_map/broadcast_in_dim | solution.py:26
  23.0 12.9 %reshape.177 = bf16[128,32896]{0,1:T(8,128)(2,1)} reshape(bf16[128,128,257]{0,2,1:T(8,128)(2,1)} %broadcast_in_dim.164) | data formatting | bytes 16842752 | tf_op jit(solution)/shard_map/reshape | solution.py:27
  35.9 7.1 %slice.26 = bf16[128,32768]{0,1:T(8,128)(2,1)} slice(bf16[128,32896]{0,1:T(8,128)(2,1)} %reshape.177), slice={[0:128], [0:32768]} | slice | bytes 16777216 | tf_op jit(solution)/shard_map/slice | solution.py:28
  43.0 12.6 %copy.37 = bf16[128,128,256]{2,1,0:T(8,128)(2,1)} copy(bf16[128,128,256]{0,2,1:T(8,128)(2,1)} %bitcast.87) | data formatting | bytes 16777216 | tf_op jit(solution)/shard_map/while | solution.py:76
  55.7 22.2 %while.38 = (s32[]{:T(128)}, f32[3,256,128,16]{1,3,2,0:T(8,128)}, bf16[3,128,128,16]{1,3,2,0:T(8,128)(2,1)S(1)}, s32[3]{0:T(128)S(1)}, s32[]{:T(128)}, /*index=5...) while((s32[]{:T(128)}, f32[3,256,128,16]{1,3,2,0:T(8,128)}, ...), condition=%wide.region_6.7_spmd, body=%wide.region_4.6_spmd.sunk | while | flops 138451200 | bytes 11081005 | solution.py:88
  57.1 6.0 %bitcast_dynamic-update-slice_fusion.2 = f32[3,256,128,16]{1,3,2,0:T(8,128)} fusion(f32[3,256,128,16]{1,3,2,0:T(8,128)} %get-tuple-element.601, s32[]{:T(128)S(6)} %copy.63, bf16[128,128,256]{2,1,0:T(8,128)(2,1)} %get-tuple-element.618, pred[128,256]{1,0:T(8,128)(4,1)S(1)} %broadcast_compare_fusion.7, ...), kind=kOutput, calls=%fused_computation.16.clone.1 | convolution fusion | flops 138412032 | bytes 11043840 | tf_op jit(solution)/shard_map/while/body/eval_jaxpr/fab,afc->bfc/dot_general | solution.py:84
  64.5 6.0 %bitcast_dynamic-update-slice_fusion.2 = f32[3,256,128,16]{1,3,2,0:T(8,128)} fusion(f32[3,256,128,16]{1,3,2,0:T(8,128)} %get-tuple-element.601, s32[]{:T(128)S(6)} %copy.63, bf16[128,128,256]{2,1,0:T(8,128)(2,1)} %get-tuple-element.618, pred[128,256]{1,0:T(8,128)(4,1)S(1)} %broadcast_compare_fusion.7, ...), kind=kOutput, calls=%fused_computation.16.clone.1 | convolution fusion | flops 138412032 | bytes 11043840 | tf_op jit(solution)/shard_map/while/body/eval_jaxpr/fab,afc->bfc/dot_general | solution.py:84
  71.9 6.0 %bitcast_dynamic-update-slice_fusion.2 = f32[3,256,128,16]{1,3,2,0:T(8,128)} fusion(f32[3,256,128,16]{1,3,2,0:T(8,128)} %get-tuple-element.601, s32[]{:T(128)S(6)} %copy.63, bf16[128,128,256]{2,1,0:T(8,128)(2,1)} %get-tuple-element.618, pred[128,256]{1,0:T(8,128)(4,1)S(1)} %broadcast_compare_fusion.7, ...), kind=kOutput, calls=%fused_computation.16.clone.1 | convolution fusion | flops 138412032 | bytes 11043840 | tf_op jit(solution)/shard_map/while/body/eval_jaxpr/fab,afc->bfc/dot_general | solution.py:84
  81.6 3.1 slice.23
  86.2 2.6 copy.35
  88.8 3.2 maximum_add_fusion
  94.3 2.7 fusion.25
  97.8 12.0 %collective-permute-start = (bf16[128,2048]{0,1:T(8,128)(2,1)}, bf16[128,2048]{0,1:T(8,128)(2,1)}, u32[]{:S(2)}, u32[]{:S(2)}) collective-permute-start(bf16[128,2048]{0,1:T(8,128)(2,1)} %slice.25), channel_id=1, source_target_pairs={{0,4},{4,8},{8,12},{12,16},{16,20},{20,24},{24,28},{1,5},{5,9},{9,... | collective-permute-start | bytes 1572872 | tf_op jit(solution)/shard_map/ppermute | solution.py:12
  119.3 5.1 %concatenate.18 = bf16[3,128,128,16]{1,0,3,2:T(4,128)(2,1)} reshape(bf16[384,2048]{0,1:T(8,128)(2,1)} %pad_maximum_fusion.1) | data formatting | bytes 3145728 | tf_op jit(solution)/shard_map/concatenate | solution.py:54
  124.5 5.6 %pad_maximum_fusion = bf16[3,256,128,16]{1,0,3,2:T(4,128)(2,1)S(1)} fusion(bf16[3,128,128,16]{1,0,3,2:T(4,128)(2,1)} %concatenate.19, bf16[3,128,128,16]{1,0,3,2:T(4,128)(2,1)} %concatenate.18), kind=kLoop, calls=%fused_computation.35 | loop fusion | flops 6291456 | bytes 6291456 | tf_op jit(solution)/shard_map/concatenate | solution.py:54
  132.2 101.7 %while.37 = (s32[]{:T(128)}, f32[3,128,128,16]{1,0,3,2:T(4,128)}, bf16[3,256,128,16]{1,3,2,0:T(8,128)(2,1)}, s32[3]{0:T(128)S(1)}, s32[]{:T(128)}, /*index=5*/s3...) while((s32[]{:T(128)}, f32[3,128,128,16]{1,0,3,2:T(4,128)}, ...), condition=%wide.region_3.4_spmd, body=%wide.region_1.3_spmd.sunk | while | flops 138451200 | bytes 12652861 | solution.py:76
  133.6 6.0 %fusion.37 = f32[128,16,128]{2,1,0:T(8,128)S(1)} fusion(bf16[128,128,256]{2,1,0:T(8,128)(2,1)} %get-tuple-element.653, pred[128,256]{1,0:T(8,128)(4,1)S(1)} %broadcast_compare_fusion.6, bf16[3,256,128,16]{1,3,2,0:T(8,128)(2,1)} %get-tuple-element.648, s32[]{:T(128)S(6)} %copy.69), kind=kOutput, calls=%fused_computation.clone.1 | convolution fusion | flops 138412032 | bytes 10518532 | tf_op jit(solution)/shard_map/while/body/eval_jaxpr/fab,bfc->afc/dot_general | solution.py:71
  139.6 26.5 %dynamic_update_slice.17 = f32[3,128,128,16]{1,0,3,2:T(4,128)} dynamic-update-slice(f32[3,128,128,16]{1,0,3,2:T(4,128)} %get-tuple-element.635, f32[1,128,128,16]{1,0,3,2:T(1,128)S(1)} %bitcast.88, s32[]{:T(128)S(6)} %copy.69, s32[]{:T(128)} %constant.120.clone.1..sunk, s32[]{:T(128)} %constant.120.clone.1..sunk, s32[]{:T(128)} %constant.120.clone.1..sunk) | dynamic-update-slice | bytes 2097156 | tf_op jit(solution)/shard_map/while/body/jit(dynamic_update_index_in_dim)/dynamic_update_slice | solution.py:76
  167.5 6.0 %fusion.37 = f32[128,16,128]{2,1,0:T(8,128)S(1)} fusion(bf16[128,128,256]{2,1,0:T(8,128)(2,1)} %get-tuple-element.653, pred[128,256]{1,0:T(8,128)(4,1)S(1)} %broadcast_compare_fusion.6, bf16[3,256,128,16]{1,3,2,0:T(8,128)(2,1)} %get-tuple-element.648, s32[]{:T(128)S(6)} %copy.69), kind=kOutput, calls=%fused_computation.clone.1 | convolution fusion | flops 138412032 | bytes 10518532 | tf_op jit(solution)/shard_map/while/body/eval_jaxpr/fab,bfc->afc/dot_general | solution.py:71
  173.5 26.5 %dynamic_update_slice.17 = f32[3,128,128,16]{1,0,3,2:T(4,128)} dynamic-update-slice(f32[3,128,128,16]{1,0,3,2:T(4,128)} %get-tuple-element.635, f32[1,128,128,16]{1,0,3,2:T(1,128)S(1)} %bitcast.88, s32[]{:T(128)S(6)} %copy.69, s32[]{:T(128)} %constant.120.clone.1..sunk, s32[]{:T(128)} %constant.120.clone.1..sunk, s32[]{:T(128)} %constant.120.clone.1..sunk) | dynamic-update-slice | bytes 2097156 | tf_op jit(solution)/shard_map/while/body/jit(dynamic_update_index_in_dim)/dynamic_update_slice | solution.py:76
  201.4 6.0 %fusion.37 = f32[128,16,128]{2,1,0:T(8,128)S(1)} fusion(bf16[128,128,256]{2,1,0:T(8,128)(2,1)} %get-tuple-element.653, pred[128,256]{1,0:T(8,128)(4,1)S(1)} %broadcast_compare_fusion.6, bf16[3,256,128,16]{1,3,2,0:T(8,128)(2,1)} %get-tuple-element.648, s32[]{:T(128)S(6)} %copy.69), kind=kOutput, calls=%fused_computation.clone.1 | convolution fusion | flops 138412032 | bytes 10518532 | tf_op jit(solution)/shard_map/while/body/eval_jaxpr/fab,bfc->afc/dot_general | solution.py:71
  207.4 26.5 %dynamic_update_slice.17 = f32[3,128,128,16]{1,0,3,2:T(4,128)} dynamic-update-slice(f32[3,128,128,16]{1,0,3,2:T(4,128)} %get-tuple-element.635, f32[1,128,128,16]{1,0,3,2:T(1,128)S(1)} %bitcast.88, s32[]{:T(128)S(6)} %copy.69, s32[]{:T(128)} %constant.120.clone.1..sunk, s32[]{:T(128)} %constant.120.clone.1..sunk, s32[]{:T(128)} %constant.120.clone.1..sunk) | dynamic-update-slice | bytes 2097156 | tf_op jit(solution)/shard_map/while/body/jit(dynamic_update_index_in_dim)/dynamic_update_slice | solution.py:76
  233.9 43.6 %while.39 = (s32[]{:T(128)}, f32[128,128,256]{2,1,0:T(8,128)}, s32[3]{0:T(128)S(1)}, s32[]{:T(128)}, s32[1,16]{1,0:T(1,128)S(1)}, /*index=5*/s32[16]{0:T(128)S(1...) while((s32[]{:T(128)}, f32[128,128,256]{2,1,0:T(8,128)}, ...), condition=%wide.region_9.10_spmd.clone, body=%wide.region_7.9_spmd.clone.sunk | while | flops 146839808 | bytes 35198780 | solution.py:101
  235.4 9.8 %select_add_fusion.2 = f32[128,128,256]{2,1,0:T(8,128)} fusion(f32[128,128,256]{2,1,0:T(8,128)} %get-tuple-element.671, pred[]{:T(512)S(6)} %compare.4, pred[128,256]{1,0:T(8,128)(4,1)S(1)} %broadcast_compare_fusion.8, bf16[3,256,128,16]{1,3,2,0:T(8,128)(2,1)} %get-tuple-element.689, s32[]{:T(128)S(6)} %copy.75, ...), kind=kOutput, calls=%fused_computation.25.clone.1 | convolution fusion | flops 146800640 | bytes 35161600 | tf_op jit(solution)/shard_map/while/body/eval_jaxpr/afc,bfc->fab/dot_general | solution.py:98
  246.6 14.7 %select_add_fusion.2 = f32[128,128,256]{2,1,0:T(8,128)} fusion(f32[128,128,256]{2,1,0:T(8,128)} %get-tuple-element.671, pred[]{:T(512)S(6)} %compare.4, pred[128,256]{1,0:T(8,128)(4,1)S(1)} %broadcast_compare_fusion.8, bf16[3,256,128,16]{1,3,2,0:T(8,128)(2,1)} %get-tuple-element.689, s32[]{:T(128)S(6)} %copy.75, ...), kind=kOutput, calls=%fused_computation.25.clone.1 | convolution fusion | flops 146800640 | bytes 35161600 | tf_op jit(solution)/shard_map/while/body/eval_jaxpr/afc,bfc->fab/dot_general | solution.py:98
  262.8 14.7 %select_add_fusion.2 = f32[128,128,256]{2,1,0:T(8,128)} fusion(f32[128,128,256]{2,1,0:T(8,128)} %get-tuple-element.671, pred[]{:T(512)S(6)} %compare.4, pred[128,256]{1,0:T(8,128)(4,1)S(1)} %broadcast_compare_fusion.8, bf16[3,256,128,16]{1,3,2,0:T(8,128)(2,1)} %get-tuple-element.689, s32[]{:T(128)S(6)} %copy.75, ...), kind=kOutput, calls=%fused_computation.25.clone.1 | convolution fusion | flops 146800640 | bytes 35161600 | tf_op jit(solution)/shard_map/while/body/eval_jaxpr/afc,bfc->fab/dot_general | solution.py:98
  277.5 17.8 %copy.49 = f32[128,128,256]{0,2,1:T(8,128)} copy(f32[128,128,256]{2,1,0:T(8,128)} %get-tuple-element.291) | data formatting | bytes 33554432 | tf_op jit(solution)/shard_map/transpose(jvp())/reshape | solution.py:28
  295.3 13.3 %pad.3 = f32[128,32896]{0,1:T(8,128)} pad(f32[128,32768]{0,1:T(8,128)} %bitcast.86, f32[]{:T(128)} %constant.121.clone.1), padding=0_0x0_128 | pad | bytes 33619972 | tf_op jit(solution)/shard_map/transpose(jvp())/pad | solution.py:28
  308.6 17.5 %reshape.182 = f32[128,128,257]{0,2,1:T(8,128)} reshape(f32[128,32896]{0,1:T(8,128)} %pad.3) | data formatting | bytes 33685504 | tf_op jit(solution)/shard_map/transpose(jvp())/reshape | solution.py:27
  326.1 6.8 %reduce_sum.49 = f32[128,257]{0,1:T(8,128)S(1)} reduce(f32[128,128,257]{0,2,1:T(8,128)} %reshape.182, f32[]{:T(128)} %constant.121.clone.1), dimensions={1}, to_apply=%region_10.11 | reduce | flops 4177792 | bytes 16974340 | tf_op jit(solution)/shard_map/transpose(jvp())/reduce_sum | solution.py:26
  333.7 2.7 fusion.23
  338.0 49.6 %all-reduce.3.cloned.1.call-done = f32[128,128]{1,0:T(8,128)} async-done(((f32[128,128]{1,0:T(8,128)}), f32[128,128]{1,0:T(8,128)}) %all-reduce.3.cloned.1.call-update) | async-done | bytes 65552 | tf_op jit(solution)/shard_map/psum | solution.py:108
  (95 shorter events, 41.7 us)
Async XLA Ops:
  7.2 3.8 copy-start.4
  7.2 380.5 %all-reduce.3.cloned.1.call-start = ((), (), s32[]{:S(2)}) async-start(), calls=%async_computation | async-start | bytes 131072 | tf_op jit(solution)/shard_map/psum | solution.py:108
  10.9 3.5 copy-start
  43.0 12.6 %copy-start.6 = (s32[16]{0:T(128)S(1)}, s32[16]{0:T(128)}, u32[]{:S(2)}) copy-start(s32[16]{0:T(128)} %param.16) | copy-start | bytes 196
  77.9 6.8 %copy-start.5 = (bf16[384,2048]{1,0:T(8,128)(2,1)S(1)}, bf16[384,2048]{1,0:T(8,128)(2,1)}, u32[]{:S(2)}) copy-start(bf16[384,2048]{1,0:T(8,128)(2,1)} %param.13) | copy-start | bytes 4718596
  80.3 8.5 %collective-permute-start.1 = (f32[128,128,16]{0,2,1:T(8,128)}, f32[128,128,16]{0,2,1:T(8,128)}, u32[]{:S(2)}, u32[]{:S(2)}) collective-permute-start(f32[128,128,16]{0,2,1:T(8,128)} %slice_bitcast_fusion), channel_id=1, source_target_pairs={{4,0},{8,4},{12,8},{16,12},{20,16},{24,20},{28,24},{5,1},{9,5},{13... | collective-permute-start | bytes 3145736 | tf_op jit(solution)/shard_map/ppermute | solution.py:12
  92.0 2.2 copy-start.2
  92.1 2.2 copy-start.3
  97.8 19.2 %collective-permute-start = (bf16[128,2048]{0,1:T(8,128)(2,1)}, bf16[128,2048]{0,1:T(8,128)(2,1)}, u32[]{:S(2)}, u32[]{:S(2)}) collective-permute-start(bf16[128,2048]{0,1:T(8,128)(2,1)} %slice.25), channel_id=1, source_target_pairs={{0,4},{4,8},{8,12},{12,16},{16,20},{20,24},{24,28},{1,5},{5,9},{9,... | collective-permute-start | bytes 1572872 | tf_op jit(solution)/shard_map/ppermute | solution.py:12
  326.1 7.5 %copy-start.1 = (bf16[384,2048]{0,1:T(8,128)(2,1)S(1)}, bf16[384,2048]{0,1:T(8,128)(2,1)}, u32[]{:S(2)}) copy-start(bf16[384,2048]{0,1:T(8,128)(2,1)} %copy-done) | copy-start | bytes 4718596
Sparse Core Ops, SparseCore 0:
  333.8 53.8 all-reduce.2
where the time goes:
time: 400 us; the launch traced here: 396 us
  local copies, waits for them, and re-layouts  209 us (52%)
  matrix products  75.2 us (19%)
  waiting for transfers between devices  49.6 us (12%)
  other arithmetic  28.6 us (7%)
  between operations  14.2 us (4%)
  starting transfers between devices  13.3 us (3%)
  loops' own time  5.97 us (1%)
    dynamic_update_slice x3, local copies, waits for them, and re-layouts, on_device(): lax.map(forward_block, (block_ids, windows)).reshape(row_count, local_width)  79.5 us
    psum x1, waiting for transfers between devices, on_device(): summed = lax.psum(filt_local, 'ctx')  49.6 us
    dot_general x3, matrix products, corr_step(): jnp.einsum('afc,bfc->fab', cot_block, window, preferred_element_type=jnp....  39.2 us
    reshape x2, local copies, waits for them, and re-layouts, band_table(): flat_rows = tiled_rows.reshape(group_count, tap_count * (2 * tap_count + 1))  30.4 us
    dot_general x3, matrix products, forward_block(): jnp.einsum('fab,bfc->afc', banded_at(block_index), window, preferred_elem...  18 us
    dot_general x3, matrix products, backward_block(): jnp.einsum('fab,afc->bfc', banded_at(block_index), cot_block, preferred_e...  17.9 us
    reshape x1, local copies, waits for them, and re-layouts, band_table(): flat_rows[:, :2 * tap_count * tap_count]  17.8 us
    while x2, local copies, waits for them, and re-layouts, on_device(): lax.map(forward_block, (block_ids, windows)).reshape(row_count, local_width)  14.8 us
  transfers between devices with their start and end apart: 3, of which 1 were waited for; matrix products, arithmetic and copies ran while one was open for 5% of the time, Pallas kernels for 0%

commit v1 on v0

v1 whole, which is shorter than its diff:
```python
import functools
import math

import jax
import jax.numpy as jnp
from jax import lax
from jax.experimental import pallas as pl
from jax.experimental.pallas import tpu as pltpu
from jax.sharding import PartitionSpec as P

BF = jnp.bfloat16
F32 = jnp.float32
CHUNK = 128


def passed_along(value, axis, steps):
    count = lax.axis_size(axis)
    first, last = (max(0, -steps), min(count, count - steps))
    return lax.ppermute(value, axis, [(source, source + steps) for source in range(first, last)])


def doc_ids(lengths_ref, first, shape, dim):
    tokens = first + lax.broadcasted_iota(jnp.int32, shape, dim)

    def add(d, carry):
        end, ids = carry
        end = end + lengths_ref[d]
        return (end, ids + jnp.where(tokens >= end, 1, 0))

    return lax.fori_loop(
        0, lengths_ref.shape[0], add, (jnp.int32(0), jnp.zeros(shape, jnp.int32)), unroll=4
    )[1]


def fill_masks(lengths_ref, row_base, fwd, bwd, mask_f, mask_b, mask_c):
    taps = CHUNK
    row = lax.broadcasted_iota(jnp.int32, (taps, taps), 0)
    col = lax.broadcasted_iota(jnp.int32, (taps, taps), 1)
    for i, n in enumerate(fwd):
        first = row_base + n * taps
        mine = doc_ids(lengths_ref, first, (taps, taps), 0)
        prev = doc_ids(lengths_ref, first - taps, (8, taps), 1)[:1]
        cur = doc_ids(lengths_ref, first, (8, taps), 1)[:1]
        left = jnp.where((mine == prev) & (col > row), 1.0, 0.0)
        right = jnp.where((mine == cur) & (col <= row), 1.0, 0.0)
        mask_f[i, :, :taps] = left.astype(BF)
        mask_f[i, :, taps:] = right.astype(BF)
        mask_c[i, :, :taps] = left
        mask_c[i, :, taps:] = right
    for i, n in enumerate(bwd):
        first = row_base + n * taps
        mine = doc_ids(lengths_ref, first, (taps, taps), 0)
        cur = doc_ids(lengths_ref, first, (8, taps), 1)[:1]
        later = doc_ids(lengths_ref, first + taps, (8, taps), 1)[:1]
        left = jnp.where((mine == cur) & (col >= row), 1.0, 0.0)
        right = jnp.where((mine == later) & (col < row), 1.0, 0.0)
        mask_b[i, :, :taps] = left.astype(BF)
        mask_b[i, :, taps:] = right.astype(BF)


def fill_taps(filters_ref, taps_f, taps_b):
    taps, count = filters_ref.shape
    row = lax.broadcasted_iota(jnp.int32, (taps, taps), 0)
    col = lax.broadcasted_iota(jnp.int32, (taps, taps), 1)
    same = jnp.where(row == col, 1.0, 0.0).astype(BF)
    flip = jnp.where(((row + col) & (taps - 1)) == 0, 1.0, 0.0).astype(BF)
    dims = (((0,), (0,)), ((), ()))
    table = filters_ref[...]
    taps_b[...] = lax.dot_general(table, same, dims, preferred_element_type=F32)
    taps_f[...] = lax.dot_general(table, flip, dims, preferred_element_type=F32)


def convolve(tap_rows, masks, inputs, chan_group):
    taps = CHUNK
    lane = lax.broadcasted_iota(jnp.int32, (taps, taps), 1)
    per = tap_rows.shape[0]
    totals = [None] * len(inputs)
    for f in range(per):
        spread = jnp.broadcast_to(tap_rows[f : f + 1], (taps, taps))
        circ = pltpu.roll(spread, 0, 1, stride=1, stride_axis=0).astype(BF)
        both = jnp.concatenate([circ, circ], axis=1)
        mine = lane >= f * chan_group
        for i, x in enumerate(inputs):
            got = jnp.dot(both * masks[i], x, preferred_element_type=F32)
            totals[i] = got if f == 0 else jnp.where(mine, got, totals[i])
    return totals


def correlate(cots, windows, masks, per, chan_group):
    taps = CHUNK
    lane = lax.broadcasted_iota(jnp.int32, (1, taps), 1)
    sums = []
    for f in range(per):
        mine = jnp.where(
            (lane >= f * chan_group) & (lane < (f + 1) * chan_group), 1.0, 0.0
        ).astype(BF)
        total = None
        for cot, window, mask in zip(cots, windows, masks):
            got = lax.dot_general(
                cot * mine, window, (((1,), (1,)), ((), ())), preferred_element_type=F32
            )
            got = got * mask[...]
            got = got[:, :taps] + got[:, taps:]
            total = got if total is None else total + got
        held = total[:8]
        for q in range(1, taps // 8):
            held = held + pltpu.roll(total[8 * q : 8 * q + 8], taps - 8 * q, 1)
        sums.append(held)
    return sums


def collapse(corr_ref, scale):
    taps = CHUNK
    total = corr_ref[:, 0, :]
    for r in range(1, 8):
        total = total + pltpu.roll(corr_ref[:, r, :], taps - r, 1)
    row = lax.broadcasted_iota(jnp.int32, (taps, taps), 0)
    col = lax.broadcasted_iota(jnp.int32, (taps, taps), 1)
    flip = jnp.where(((row + col) & (taps - 1)) == 0, scale, 0.0)
    return lax.dot_general(
        flip, total, (((1,), (1,)), ((), ())),
        precision=lax.Precision.HIGHEST, preferred_element_type=F32,
    )


def inner_kernel(
    blocks, chan_group, base_ref, lengths_ref, filters_ref, gate_ref, key_ref, value_ref, cot_ref,
    gg_ref, kg_ref, vg_ref, corr_ref, taps_f, taps_b, mask_f, mask_b, mask_c,
):
    taps = CHUNK
    fwd, bwd = range(1, blocks), range(0, blocks - 1)

    @pl.when(pl.program_id(0) == 0)
    def _():
        fill_taps(filters_ref, taps_f, taps_b)
        fill_masks(lengths_ref, base_ref[0], fwd, bwd, mask_f, mask_b, mask_c)

    per = CHUNK // chan_group
    here = pl.ds(pl.multiple_of(pl.program_id(0) * per, per), per)
    key = key_ref[...].astype(F32)
    value = value_ref[...].astype(F32)
    cot = cot_ref[...].astype(F32)
    product = (key * value).astype(BF)
    filt_cot = (cot * gate_ref[...].astype(F32)).astype(BF)
    windows = [product[(n - 1) * taps : (n + 1) * taps] for n in fwd]
    outs = convolve(taps_f[here], [mask_f.at[i][...] for i in range(len(fwd))], windows, chan_group)
    for n, out in zip(fwd, outs):
        rows = slice(n * taps, (n + 1) * taps)
        gg_ref[rows] = (cot[rows] * out).astype(BF)
    ahead = [filt_cot[n * taps : (n + 2) * taps] for n in bwd]
    outs = convolve(taps_b[here], [mask_b.at[i][...] for i in range(len(bwd))], ahead, chan_group)
    for n, out in zip(bwd, outs):
        rows = slice(n * taps, (n + 1) * taps)
        kg_ref[rows] = (out * value[rows]).astype(BF)
        vg_ref[rows] = (out * key[rows]).astype(BF)
    cots = [filt_cot[n * taps : (n + 1) * taps] for n in fwd]
    sums = correlate(cots, windows, [mask_c.at[i] for i in range(len(fwd))], per, chan_group)
    for f in range(per):
        corr_ref[pl.program_id(0) * per + f] = sums[f]


def edge_kernel(
    blocks, chan_group, scale, base_ref, lengths_ref, filters_ref, prev_ref, next_ref,
    key_ref, value_ref, key_last, value_last, gate_ref, cot_ref, gate_last, cot_last,
    part_ref, gg_in, kg_in, vg_in,
    gg_ref, kg_ref, vg_ref, grad_ref, taps_f, taps_b, mask_f, mask_b, mask_c, corr_ref,
):
    taps = CHUNK
    steps = pl.num_programs(0)

    @pl.when(pl.program_id(0) == 0)
    def _():
        fill_taps(filters_ref, taps_f, taps_b)
        fill_masks(lengths_ref, base_ref[0], [0], [blocks - 1], mask_f, mask_b, mask_c)

    per = CHUNK // chan_group
    here = pl.ds(pl.multiple_of(pl.program_id(0) * per, per), per)
    cot = cot_ref[...].astype(F32)
    product = (key_ref[...].astype(F32) * value_ref[...].astype(F32)).astype(BF)
    filt_cot = (cot * gate_ref[...].astype(F32)).astype(BF)
    window = jnp.concatenate([prev_ref[...], product], axis=0)
    out = convolve(taps_f[here], [mask_f[0]], [window], chan_group)[0]
    gg_ref[...] = (cot * out).astype(BF)
    last_cot = (cot_last[...].astype(F32) * gate_last[...].astype(F32)).astype(BF)
    ahead = jnp.concatenate([last_cot, next_ref[...]], axis=0)
    out = convolve(taps_b[here], [mask_b[0]], [ahead], chan_group)[0]
    kg_ref[...] = (out * value_last[...].astype(F32)).astype(BF)
    vg_ref[...] = (out * key_last[...].astype(F32)).astype(BF)
    sums = correlate([filt_cot], [window], [mask_c.at[0]], per, chan_group)
    for f in range(per):
        at = pl.program_id(0) * per + f
        corr_ref[at] = part_ref[at] + sums[f]

    @pl.when(pl.program_id(0) == steps - 1)
    def _():
        grad_ref[...] = collapse(corr_ref, scale)


def on_device(gate, key, value, filters, lengths, cotangent):
    row_count, width = gate.shape
    taps, filt_count = filters.shape
    chan_group = width // filt_count
    blocks = row_count // taps
    ctx_count = lax.axis_size("ctx")
    base = (lax.axis_index("ctx") * row_count).astype(jnp.int32).reshape(1)
    scale = 1.0 / math.sqrt(row_count * ctx_count)
    tail = slice(row_count - taps, row_count)
    prev = passed_along(
        (key[tail].astype(F32) * value[tail].astype(F32)).astype(BF), "ctx", 1
    )
    later = passed_along(
        (cotangent[:taps].astype(F32) * gate[:taps].astype(F32)).astype(BF), "ctx", -1
    )
    steps = width // CHUNK
    smem = pl.BlockSpec(memory_space=pltpu.SMEM)
    whole = pl.BlockSpec((taps, filt_count), lambda g: (0, 0))
    strip = pl.BlockSpec((row_count, CHUNK), lambda g: (0, g))
    top = pl.BlockSpec((taps, CHUNK), lambda g: (0, g))
    bottom = pl.BlockSpec((taps, CHUNK), lambda g: (blocks - 1, g))
    table = pl.BlockSpec((filt_count, 8, taps), lambda g: (0, 0, 0))
    anywhere = pl.BlockSpec(memory_space=pl.ANY)
    full = jax.ShapeDtypeStruct((row_count, width), BF)

    def scratch(count):
        return [
            pltpu.VMEM((filt_count, taps), F32),
            pltpu.VMEM((filt_count, taps), F32),
            pltpu.VMEM((count, taps, 2 * taps), BF),
            pltpu.VMEM((count, taps, 2 * taps), BF),
            pltpu.VMEM((count, taps, 2 * taps), F32),
        ]

    work = 3 * 2 * row_count * 2 * taps * width
    gate_grad, key_grad, value_grad, part = pl.pallas_call(
        functools.partial(inner_kernel, blocks, chan_group),
        grid=(steps,),
        in_specs=[smem, smem, whole, strip, strip, strip, strip],
        out_specs=[strip, strip, strip, table],
        out_shape=[full, full, full, jax.ShapeDtypeStruct((filt_count, 8, taps), F32)],
        scratch_shapes=scratch(blocks - 1),
        compiler_params=pltpu.CompilerParams(vmem_limit_bytes=32 * 2**20),
        cost_estimate=pl.CostEstimate(
            flops=16 * work, bytes_accessed=7 * 2 * row_count * width, transcendentals=0
        ),
        name="inner",
    )(base, lengths, filters, gate, key, value, cotangent)
    gate_grad, key_grad, value_grad, local = pl.pallas_call(
        functools.partial(edge_kernel, blocks, chan_group, scale),
        grid=(steps,),
        in_specs=[smem, smem, whole, top, top, top, top, bottom, bottom, top, top, bottom, bottom]
        + [table, anywhere, anywhere, anywhere],
        out_specs=[top, bottom, bottom, whole],
        out_shape=[full, full, full, jax.ShapeDtypeStruct((taps, filt_count), F32)],
        scratch_shapes=scratch(1) + [pltpu.VMEM((filt_count, 8, taps), F32)],
        input_output_aliases={14: 0, 15: 1, 16: 2},
        compiler_params=pltpu.CompilerParams(vmem_limit_bytes=32 * 2**20),
        cost_estimate=pl.CostEstimate(
            flops=8 * work, bytes_accessed=4 * 2 * row_count * width, transcendentals=0
        ),
        name="edge",
    )(
        base, lengths, filters, prev, later, key, value, key, value,
        gate, cotangent, gate, cotangent, part, gate_grad, key_grad, value_grad,
    )
    filter_grad = lax.psum_scatter(local, "ctx", scatter_dimension=0, tiled=True)
    return (gate_grad, key_grad, value_grad, filter_grad)


def solution(mesh):
    return jax.shard_map(
        on_device,
        mesh=mesh,
        in_specs=(
            P("ctx", "tp"),
            P("ctx", "tp"),
            P("ctx", "tp"),
            P(None, "tp"),
            P(),
            P("ctx", "tp"),
        ),
        out_specs=(P("ctx", "tp"), P("ctx", "tp"), P("ctx", "tp"), P("ctx", "tp")),
        check_vma=False,
    )
```

time: 400 us -> 103 us (0.26)
  local copies, waits for them, and re-layouts: 209 us -> 3.58 us
  matrix products: 75.2 us -> 0 us
  Pallas kernels: 0 us -> 38.6 us
  other arithmetic: 28.6 us -> 4.44 us
  waiting for transfers between devices: 49.6 us -> 37.2 us
  starting transfers between devices: 13.3 us -> 4.46 us
  loops' own time: 5.97 us -> 0 us
    dynamic_update_slice x3 -> x0, local copies, waits for them, and re-layouts: 79.5 us -> none  [on_device(): lax.map(forward_block, (block_ids, windows)).reshape(row_count, local_width)]
    dot_general x9 -> x0, matrix products: 75.2 us -> none  [the longest x3 39.2 us: corr_step(): jnp.einsum('afc,bfc->fab', cot_block, window, preferred_element_type=jnp....]
    reshape x4 -> x0, local copies, waits for them, and re-layouts: 50.3 us -> none  [the longest x2 30.4 us: band_table(): flat_rows = tiled_rows.reshape(group_count, tap_count * (2 * tap_count + 1))]
    psum x1 -> x0, waiting for transfers between devices: 49.6 us -> none  [on_device(): summed = lax.psum(filt_local, 'ctx')]
    pallas_call x0 -> x2, Pallas kernels: none -> 38.6 us  [the longest x1 22.3 us: on_device(): pl.pallas_call(functools.partial(inner_kernel, blocks, chan_group), grid=...]
    reduce_scatter x0 -> x1, waiting for transfers between devices: none -> 37.2 us  [on_device(): lax.psum_scatter(local, 'ctx', scatter_dimension=0, tiled=True)]
    while x3 -> x0, local copies, waits for them, and re-layouts: 16.6 us -> none  [the longest x2 14.8 us: on_device(): lax.map(forward_block, (block_ids, windows)).reshape(row_count, local_width)]
    pad x1 -> x0, local copies, waits for them, and re-layouts: 13.3 us -> none  [band_table(): flat_rows[:, :2 * tap_count * tap_count]]
  transfers between devices with their start and end apart: 3 -> 3, of which waited for: 1 -> 1; matrix products, arithmetic and copies ran while one was open for 5% -> 2% of each run, Pallas kernels for 0% -> 22%
where the time goes in v1:
time: 103 us; the launch traced here: 102 us
  Pallas kernels  38.6 us (37%)
  waiting for transfers between devices  37.2 us (36%)
  between operations  14.1 us (14%)
  starting transfers between devices  4.46 us (4%)
  other arithmetic  4.44 us (4%)
  local copies, waits for them, and re-layouts  3.58 us (3%)
    reduce_scatter x1, waiting for transfers between devices, on_device(): lax.psum_scatter(local, 'ctx', scatter_dimension=0, tiled=True)  37.2 us
    pallas_call x1, Pallas kernels, on_device(): pl.pallas_call(functools.partial(inner_kernel, blocks, chan_group), grid=...  22.3 us
    pallas_call x1, Pallas kernels, on_device(): pl.pallas_call(functools.partial(edge_kernel, blocks, chan_group, scale),...  16.3 us
    ppermute x2, starting transfers between devices, passed_along(): lax.ppermute(value, axis, [(source, source + steps) for source in range(f...  4.43 us
    unnamed x12, local copies, waits for them, and re-layouts  3.58 us
    convert_element_type x1, other arithmetic, on_device(): (key[tail].astype(F32) * value[tail].astype(F32)).astype(BF)  2.32 us
    convert_element_type x1, other arithmetic, on_device(): (cotangent[:taps].astype(F32) * gate[:taps].astype(F32)).astype(BF)  2.13 us
  transfers between devices with their start and end apart: 3, of which 1 were waited for; matrix products, arithmetic and copies ran while one was open for 2% of the time, Pallas kernels for 22%

profile of v1, /device:TPU:0, one launch (start us, length us, event | category | flops | bytes accessed | tf_op | source)
XLA Modules:
  0.0 102.4 jit_solution(3002986229586574472)
XLA Ops:
  7.2 0.0 copy-start
  7.2 0.0 copy-start.1
  7.2 0.0 copy-start.5
  7.2 0.0 reduce-scatter.2.cloned.1.call-start
  7.2 2.3 %multiply_convert_fusion.1 = bf16[128,2048]{1,0:T(8,128)(2,1)} fusion(bf16[384,2048]{1,0:T(8,128)(2,1)} %value_last.1, bf16[384,2048]{1,0:T(8,128)(2,1)} %key_last.1), kind=kLoop, calls=%fused_computation.1 | loop fusion | flops 1048576 | bytes 1572864 | tf_op jit(solution)/shard_map/convert_element_type | solution.py:209
  9.6 3.1 %collective-permute-start = (bf16[128,2048]{1,0:T(8,128)(2,1)}, bf16[128,2048]{1,0:T(8,128)(2,1)}, u32[]{:S(2)}, u32[]{:S(2)}) collective-permute-start(bf16[128,2048]{1,0:T(8,128)(2,1)} %multiply_convert_fusion.1), channel_id=1, source_target_pairs={{0,4},{4,8},{8,12},{12,16},{16,20},{20,24},{24,28},{1,5},{5,9},{9,... | collective-permute-start | bytes 1572872 | tf_op jit(solution)/shard_map/ppermute | solution.py:19
  12.7 2.1 %multiply_convert_fusion = bf16[128,2048]{1,0:T(8,128)(2,1)} fusion(bf16[384,2048]{1,0:T(8,128)(2,1)} %gate_last.1, bf16[384,2048]{1,0:T(8,128)(2,1)} %cot_last.1), kind=kLoop, calls=%fused_computation | loop fusion | flops 1048576 | bytes 1572864 | tf_op jit(solution)/shard_map/convert_element_type | solution.py:212
  14.8 1.3 %collective-permute-start.1 = (bf16[128,2048]{1,0:T(8,128)(2,1)}, bf16[128,2048]{1,0:T(8,128)(2,1)}, u32[]{:S(2)}, u32[]{:S(2)}) collective-permute-start(bf16[128,2048]{1,0:T(8,128)(2,1)} %multiply_convert_fusion), channel_id=1, source_target_pairs={{4,0},{8,4},{12,8},{16,12},{20,16},{24,20},{28,24},{5,1},{9,5},{13... | collective-permute-start | bytes 1572872 | tf_op jit(solution)/shard_map/ppermute | solution.py:19
  16.1 0.0 copy-done
  16.1 0.0 copy-done.1
  16.1 0.0 copy-done.5
  16.2 0.0 copy-start.2
  16.2 1.4 %copy-done.2 = bf16[384,2048]{1,0:T(8,128)(2,1)S(1)} copy-done((bf16[384,2048]{1,0:T(8,128)(2,1)S(1)}, bf16[384,2048]{1,0:T(8,128)(2,1)}, u32[]{:S(2)}) %copy-start.2) | copy-done | bytes 1572888
  17.6 0.0 copy-start.3
  17.6 1.4 %copy-done.3 = bf16[384,2048]{1,0:T(8,128)(2,1)S(1)} copy-done((bf16[384,2048]{1,0:T(8,128)(2,1)S(1)}, bf16[384,2048]{1,0:T(8,128)(2,1)}, u32[]{:S(2)}) %copy-start.3) | copy-done | bytes 1572888
  19.0 0.0 copy-start.4
  19.0 0.8 copy-done.4
  19.7 22.3 %inner.1 = (bf16[384,2048]{1,0:T(8,128)(2,1)}, bf16[384,2048]{1,0:T(8,128)(2,1)}, bf16[384,2048]{1,0:T(8,128)(2,1)}, f32[128,8,128]{2,1,0:T(8,128)S(1)}) custom-call(s32[1]{0:T(128)} %bitcast.base_ref, s32[16]{0:T(128)S(1)} %copy-done.5, bf16[128,128]{1,0:T(8,128)(2,1)S(1)} %copy-done.4, bf16[384,2048]{1,0:T(8,128)(2,1)S(1)} %copy-done.2, ...), custom_call_target="tpu_custom_call" | custom-call | flops 19327352832 | bytes 11010048 | tf_op jit(solution)/shard_map/inner/pallas_call | solution.py:234
  42.1 0.0 collective-permute-done.prev_ref
  42.1 0.0 collective-permute-done.1.next_ref
  42.1 16.3 %edge.1 = (bf16[384,2048]{1,0:T(8,128)(2,1)}, bf16[384,2048]{1,0:T(8,128)(2,1)}, bf16[384,2048]{1,0:T(8,128)(2,1)}, f32[128,128]{1,0:T(8,128)}) custom-call(s32[1]{0:T(128)} %bitcast.base_ref, s32[16]{0:T(128)S(1)} %copy-done.5, bf16[128,128]{1,0:T(8,128)(2,1)S(1)} %copy-done.4, ...), custom_call_target="tpu_custom_call", output_to_operand_aliasing={{0}: (14, {}), {1}: (15, {}), {2}: (16, {})} | custom-call | flops 9663676416 | bytes 6291456 | tf_op jit(solution)/shard_map/edge/pallas_call | solution.py:247
  58.4 0.0 reduce-scatter.2.cloned.1.call-update
  58.4 37.2 %reduce-scatter.2.cloned.1.call-done = f32[16,128]{1,0:T(8,128)} async-done(((f32[128,128]{1,0:T(8,128)}), f32[16,128]{1,0:T(8,128)}) %reduce-scatter.2.cloned.1.call-update) | async-done | bytes 8208 | tf_op jit(solution)/shard_map/reduce_scatter | solution.py:265
Async XLA Ops:
  7.2 9.0 %copy-start = (bf16[384,2048]{1,0:T(8,128)(2,1)S(1)}, bf16[384,2048]{1,0:T(8,128)(2,1)}, u32[]{:S(2)}) copy-start(bf16[384,2048]{1,0:T(8,128)(2,1)} %value_last.1) | copy-start | bytes 4718596
  7.2 9.0 %copy-start.1 = (bf16[384,2048]{1,0:T(8,128)(2,1)S(1)}, bf16[384,2048]{1,0:T(8,128)(2,1)}, u32[]{:S(2)}) copy-start(bf16[384,2048]{1,0:T(8,128)(2,1)} %key_last.1) | copy-start | bytes 4718596
  7.2 9.0 %copy-start.5 = (s32[16]{0:T(128)S(1)}, s32[16]{0:T(128)}, u32[]{:S(2)}) copy-start(s32[16]{0:T(128)} %lengths_ref.3) | copy-start | bytes 196
  7.2 88.4 %reduce-scatter.2.cloned.1.call-start = ((), (), s32[]{:S(2)}) async-start(), calls=%async_computation.1 | async-start | bytes 73728 | tf_op jit(solution)/shard_map/reduce_scatter | solution.py:265
  9.6 32.5 %collective-permute-start = (bf16[128,2048]{1,0:T(8,128)(2,1)}, bf16[128,2048]{1,0:T(8,128)(2,1)}, u32[]{:S(2)}, u32[]{:S(2)}) collective-permute-start(bf16[128,2048]{1,0:T(8,128)(2,1)} %multiply_convert_fusion.1), channel_id=1, source_target_pairs={{0,4},{4,8},{8,12},{12,16},{16,20},{20,24},{24,28},{1,5},{5,9},{9,... | collective-permute-start | bytes 1572872 | tf_op jit(solution)/shard_map/ppermute | solution.py:19
  14.8 27.2 %collective-permute-start.1 = (bf16[128,2048]{1,0:T(8,128)(2,1)}, bf16[128,2048]{1,0:T(8,128)(2,1)}, u32[]{:S(2)}, u32[]{:S(2)}) collective-permute-start(bf16[128,2048]{1,0:T(8,128)(2,1)} %multiply_convert_fusion), channel_id=1, source_target_pairs={{4,0},{8,4},{12,8},{16,12},{20,16},{24,20},{28,24},{5,1},{9,5},{13... | collective-permute-start | bytes 1572872 | tf_op jit(solution)/shard_map/ppermute | solution.py:19
  16.2 1.4 %copy-start.2 = (bf16[384,2048]{1,0:T(8,128)(2,1)S(1)}, bf16[384,2048]{1,0:T(8,128)(2,1)}, u32[]{:S(2)}) copy-start(bf16[384,2048]{1,0:T(8,128)(2,1)} %gate_last.1) | copy-start | bytes 4718596
  17.6 1.4 %copy-start.3 = (bf16[384,2048]{1,0:T(8,128)(2,1)S(1)}, bf16[384,2048]{1,0:T(8,128)(2,1)}, u32[]{:S(2)}) copy-start(bf16[384,2048]{1,0:T(8,128)(2,1)} %cot_last.1) | copy-start | bytes 4718596
  19.0 0.8 copy-start.4
Sparse Core Ops, SparseCore 0:
  58.5 36.9 reduce-scatter.1

commit v2 on v1

v2 whole, which is shorter than its diff:
```python
import functools
import math

import jax
import jax.numpy as jnp
from jax import lax
from jax.experimental import pallas as pl
from jax.experimental.pallas import tpu as pltpu
from jax.sharding import PartitionSpec as P

BF = jnp.bfloat16
F32 = jnp.float32
CHUNK = 128


def doc_ids(lengths_ref, first, shape, dim):
    tokens = first + lax.broadcasted_iota(jnp.int32, shape, dim)

    def add(d, carry):
        end, ids = carry
        end = end + lengths_ref[d]
        return (end, ids + jnp.where(tokens >= end, 1, 0))

    return lax.fori_loop(
        0, lengths_ref.shape[0], add, (jnp.int32(0), jnp.zeros(shape, jnp.int32)), unroll=4
    )[1]


def fill_taps(filters_ref, taps_f, taps_b):
    taps, count = filters_ref.shape
    row = lax.broadcasted_iota(jnp.int32, (taps, taps), 0)
    col = lax.broadcasted_iota(jnp.int32, (taps, taps), 1)
    same = jnp.where(row == col, 1.0, 0.0).astype(BF)
    flip = jnp.where(((row + col) & (taps - 1)) == 0, 1.0, 0.0).astype(BF)
    dims = (((0,), (0,)), ((), ()))
    table = filters_ref[...]
    taps_b[...] = lax.dot_general(table, same, dims, preferred_element_type=F32)
    taps_f[...] = lax.dot_general(table, flip, dims, preferred_element_type=F32)


def band_masks(lengths_ref, first, forward):
    taps = CHUNK
    row = lax.broadcasted_iota(jnp.int32, (taps, taps), 0)
    col = lax.broadcasted_iota(jnp.int32, (taps, taps), 1)
    mine = doc_ids(lengths_ref, first, (taps, taps), 0)
    low = first - taps if forward else first
    near = doc_ids(lengths_ref, low, (8, taps), 1)[:1]
    far = doc_ids(lengths_ref, low + taps, (8, taps), 1)[:1]
    if forward:
        bands = (col > row, col <= row)
    else:
        bands = (col >= row, col < row)
    left = jnp.where((mine == near) & bands[0], 1.0, 0.0)
    right = jnp.where((mine == far) & bands[1], 1.0, 0.0)
    return left, right


def convolve(tap_rows, mask_ref, lhs_ref, inputs, chan_group):
    taps = CHUNK
    lane = lax.broadcasted_iota(jnp.int32, (taps, taps), 1)
    per = tap_rows.shape[0]
    for f in range(per):
        spread = jnp.broadcast_to(tap_rows[f : f + 1], (taps, taps))
        circ = pltpu.roll(spread, 0, 1, stride=1, stride_axis=0).astype(BF)
        for i in range(len(inputs)):
            lhs_ref[i, f * taps : (f + 1) * taps, :taps] = circ * mask_ref[i, :, :taps]
            lhs_ref[i, f * taps : (f + 1) * taps, taps:] = circ * mask_ref[i, :, taps:]
    outs = []
    for i, x in enumerate(inputs):
        got = jnp.dot(lhs_ref[i], x, preferred_element_type=F32)
        total = got[:taps]
        for f in range(1, per):
            total = jnp.where(lane >= f * chan_group, got[f * taps : (f + 1) * taps], total)
        outs.append(total)
    return outs


def correlate(cots, windows, masks, chan_group):
    taps = CHUNK
    lane = lax.broadcasted_iota(jnp.int32, (1, taps), 1)
    per = taps // chan_group
    totals = [None] * per
    picks = [
        jnp.where((lane >= f * chan_group) & (lane < (f + 1) * chan_group), 1.0, 0.0).astype(BF)
        for f in range(per)
    ]
    for cot, window, mask in zip(cots, windows, masks):
        stacked = jnp.concatenate([cot * pick for pick in picks], axis=0)
        every = lax.dot_general(
            stacked, window, (((1,), (1,)), ((), ())), preferred_element_type=F32
        )
        for f in range(per):
            got = every[f * taps : (f + 1) * taps] * mask[...]
            got = got[:, :taps] + got[:, taps:]
            totals[f] = got if totals[f] is None else totals[f] + got
    sums = []
    for total in totals:
        held = total[:8]
        for q in range(1, taps // 8):
            held = held + pltpu.roll(total[8 * q : 8 * q + 8], taps - 8 * q, 1)
        sums.append(held)
    return sums


def collapse(corr_ref, scale):
    taps = CHUNK
    total = corr_ref[:, 0, :]
    for r in range(1, 8):
        total = total + pltpu.roll(corr_ref[:, r, :], taps - r, 1)
    row = lax.broadcasted_iota(jnp.int32, (taps, taps), 0)
    col = lax.broadcasted_iota(jnp.int32, (taps, taps), 1)
    flip = jnp.where(((row + col) & (taps - 1)) == 0, scale, 0.0)
    return lax.dot_general(
        flip, total, (((1,), (1,)), ((), ())),
        precision=lax.Precision.HIGHEST, preferred_element_type=F32,
    )


def exchange_kernel(
    n, blocks, chan_group, scale, lengths_ref, gate_ref, key_ref, value_ref, cot_ref,
    key_tail, value_tail, gate_head, cot_head,
    prev_ref, later_ref, grad_ref,
    send_p, send_c, got_p, got_c, tops, mask_c, corr_ref, local_ref, parts_ref,
    halo_send, halo_recv, part_send, part_recv,
):
    taps = CHUNK
    step = pl.program_id(0)
    steps = pl.num_programs(0) // 2
    per = CHUNK // chan_group
    me = lax.axis_index("ctx")
    share = taps // n

    def halo(source, target, slot, peer):
        return pltpu.make_async_remote_copy(
            src_ref=source,
            dst_ref=target,
            send_sem=halo_send.at[slot],
            recv_sem=halo_recv.at[slot],
            device_id={"ctx": peer},
            device_id_type=pl.DeviceIdType.MESH,
        )

    right, left = lax.rem(me + 1, n), lax.rem(me + n - 1, n)

    @pl.when(step == 0)
    def _():
        barrier = pltpu.get_barrier_semaphore()
        for k in range(1, n):
            pl.semaphore_signal(
                barrier,
                inc=1,
                device_id={"ctx": lax.rem(me + k, n)},
                device_id_type=pl.DeviceIdType.MESH,
            )
        send_p[...] = (key_tail[...].astype(F32) * value_tail[...].astype(F32)).astype(BF)
        send_c[...] = (cot_head[...].astype(F32) * gate_head[...].astype(F32)).astype(BF)
        pl.semaphore_wait(barrier, n - 1)

        @pl.when(me < n - 1)
        def _():
            halo(send_p, got_p, 0, right).start()

        @pl.when(me > 0)
        def _():
            halo(send_c, got_c, 1, left).start()

        @pl.when(me == 0)
        def _():
            got_p[...] = jnp.zeros_like(got_p)

        @pl.when(me == n - 1)
        def _():
            got_c[...] = jnp.zeros_like(got_c)

        for i in range(blocks):
            first = (me * blocks + i) * taps
            mask_c[i, :, :taps], mask_c[i, :, taps:] = band_masks(lengths_ref, first, True)

    @pl.when(step < steps)
    def _():
        product = (key_ref[...].astype(F32) * value_ref[...].astype(F32)).astype(BF)
        filt_cot = (
            cot_ref[taps:].astype(F32) * gate_ref[taps:].astype(F32)
        ).astype(BF)
        tops[step] = product[:taps]
        inner = range(1, blocks)
        cots = [filt_cot[(i - 1) * taps : i * taps] for i in inner]
        windows = [product[(i - 1) * taps : (i + 1) * taps] for i in inner]
        sums = correlate(cots, windows, [mask_c.at[i] for i in inner], chan_group)
        for f in range(per):
            corr_ref[step * per + f] = sums[f]

    @pl.when(step == steps)
    def _():
        @pl.when(me < n - 1)
        def _():
            halo(send_p, got_p, 0, right).wait_send()
            halo(send_c, got_c, 1, right).wait_recv()

        @pl.when(me > 0)
        def _():
            halo(send_c, got_c, 1, left).wait_send()
            halo(send_p, got_p, 0, left).wait_recv()

        prev_ref[...] = got_p[...]
        later_ref[...] = got_c[...]

    @pl.when(step >= steps)
    def _():
        g = step - steps
        lanes = pl.ds(pl.multiple_of(g * CHUNK, CHUNK), CHUNK)
        window = jnp.concatenate([got_p[:, lanes], tops[g]], axis=0)
        sums = correlate([send_c[:, lanes]], [window], [mask_c.at[0]], chan_group)
        for f in range(per):
            corr_ref[g * per + f] = corr_ref[g * per + f] + sums[f]

    @pl.when(step == 2 * steps - 1)
    def _():
        local = collapse(corr_ref, scale)
        for i in range(n):
            local_ref[i] = local[i * share : (i + 1) * share]

        def part(k):
            peer = lax.rem(me + k, n)
            return pltpu.make_async_remote_copy(
                src_ref=local_ref.at[peer],
                dst_ref=parts_ref.at[k],
                send_sem=part_send.at[k],
                recv_sem=part_recv.at[k],
                device_id={"ctx": peer},
                device_id_type=pl.DeviceIdType.MESH,
            )

        for k in range(1, n):
            part(k).start()
        total = local_ref[me]
        for k in range(1, n):
            part(k).wait()
            total = total + parts_ref[k]
        grad_ref[...] = total


def filter_kernel(
    blocks, chan_group, base_ref, lengths_ref, filters_ref, gate_ref, key_ref, value_ref, cot_ref,
    prev_ref, later_ref,
    gg_ref, kg_ref, vg_ref, taps_f, taps_b, mask_f, mask_b, lhs_f, lhs_b,
):
    taps = CHUNK

    @pl.when(pl.program_id(0) == 0)
    def _():
        fill_taps(filters_ref, taps_f, taps_b)
        for i in range(blocks):
            first = base_ref[0] + i * taps
            for mask, forward in ((mask_f, True), (mask_b, False)):
                left, right = band_masks(lengths_ref, first, forward)
                mask[i, :, :taps] = left.astype(BF)
                mask[i, :, taps:] = right.astype(BF)

    per = CHUNK // chan_group
    here = pl.ds(pl.multiple_of(pl.program_id(0) * per, per), per)
    key = key_ref[...].astype(F32)
    value = value_ref[...].astype(F32)
    cot = cot_ref[...].astype(F32)
    product = jnp.concatenate([prev_ref[...], (key * value).astype(BF)], axis=0)
    filt_cot = jnp.concatenate(
        [(cot * gate_ref[...].astype(F32)).astype(BF), later_ref[...]], axis=0
    )
    windows = [product[i * taps : (i + 2) * taps] for i in range(blocks)]
    outs = convolve(taps_f[here], mask_f, lhs_f, windows, chan_group)
    for i, out in enumerate(outs):
        rows = slice(i * taps, (i + 1) * taps)
        gg_ref[rows] = (cot[rows] * out).astype(BF)
    ahead = [filt_cot[i * taps : (i + 2) * taps] for i in range(blocks)]
    outs = convolve(taps_b[here], mask_b, lhs_b, ahead, chan_group)
    for i, out in enumerate(outs):
        rows = slice(i * taps, (i + 1) * taps)
        kg_ref[rows] = (out * value[rows]).astype(BF)
        vg_ref[rows] = (out * key[rows]).astype(BF)


def on_device(gate, key, value, filters, lengths, cotangent):
    row_count, width = gate.shape
    taps, filt_count = filters.shape
    chan_group = width // filt_count
    blocks = row_count // taps
    ctx_count = lax.axis_size("ctx")
    share = taps // ctx_count
    base = (lax.axis_index("ctx") * row_count).astype(jnp.int32).reshape(1)
    scale = 1.0 / math.sqrt(row_count * ctx_count)
    steps = width // CHUNK
    per = CHUNK // chan_group
    smem = pl.BlockSpec(memory_space=pltpu.SMEM)
    strip = pl.BlockSpec((row_count, CHUNK), lambda g: (0, g))
    once = pl.BlockSpec((row_count, CHUNK), lambda g: (0, jnp.minimum(g, steps - 1)))
    head = pl.BlockSpec((taps, width), lambda g: (0, 0))
    bottom = pl.BlockSpec((taps, width), lambda g: (blocks - 1, 0))
    top = pl.BlockSpec((taps, CHUNK), lambda g: (0, g))
    full = jax.ShapeDtypeStruct((row_count, width), BF)
    edge = jax.ShapeDtypeStruct((taps, width), BF)
    wide = pltpu.VMEM((taps, width), BF)
    prev, later, filter_grad = pl.pallas_call(
        functools.partial(exchange_kernel, ctx_count, blocks, chan_group, scale),
        grid=(2 * steps,),
        in_specs=[smem, once, once, once, once, bottom, bottom, head, head],
        out_specs=[head, head, pl.BlockSpec((share, filt_count), lambda g: (0, 0))],
        out_shape=[edge, edge, jax.ShapeDtypeStruct((share, filt_count), F32)],
        scratch_shapes=[
            wide, wide, wide, wide,
            pltpu.VMEM((steps, taps, CHUNK), BF),
            pltpu.VMEM((blocks, taps, 2 * taps), F32),
            pltpu.VMEM((filt_count, 8, taps), F32),
            pltpu.VMEM((ctx_count, share, filt_count), F32),
            pltpu.VMEM((ctx_count, share, filt_count), F32),
            pltpu.SemaphoreType.DMA((2,)),
            pltpu.SemaphoreType.DMA((2,)),
            pltpu.SemaphoreType.DMA((ctx_count,)),
            pltpu.SemaphoreType.DMA((ctx_count,)),
        ],
        compiler_params=pltpu.CompilerParams(
            vmem_limit_bytes=40 * 2**20, collective_id=0, has_side_effects=True
        ),
        name="exchange",
    )(lengths, gate, key, value, cotangent, key, value, gate, cotangent)
    gate_grad, key_grad, value_grad = pl.pallas_call(
        functools.partial(filter_kernel, blocks, chan_group),
        grid=(steps,),
        in_specs=[
            smem, smem, pl.BlockSpec((taps, filt_count), lambda g: (0, 0)),
            strip, strip, strip, strip, top, top,
        ],
        out_specs=[strip, strip, strip],
        out_shape=[full, full, full],
        scratch_shapes=[
            pltpu.VMEM((filt_count, taps), F32),
            pltpu.VMEM((filt_count, taps), F32),
            pltpu.VMEM((blocks, taps, 2 * taps), BF),
            pltpu.VMEM((blocks, taps, 2 * taps), BF),
            pltpu.VMEM((blocks, per * taps, 2 * taps), BF),
            pltpu.VMEM((blocks, per * taps, 2 * taps), BF),
        ],
        compiler_params=pltpu.CompilerParams(vmem_limit_bytes=40 * 2**20),
        name="filter",
    )(base, lengths, filters, gate, key, value, cotangent, prev, later)
    return (gate_grad, key_grad, value_grad, filter_grad)


def solution(mesh):
    return jax.shard_map(
        on_device,
        mesh=mesh,
        in_specs=(
            P("ctx", "tp"),
            P("ctx", "tp"),
            P("ctx", "tp"),
            P(None, "tp"),
            P(),
            P("ctx", "tp"),
        ),
        out_specs=(P("ctx", "tp"), P("ctx", "tp"), P("ctx", "tp"), P("ctx", "tp")),
        check_vma=False,
    )
```

time: 103 us -> 59.1 us (0.57)
  waiting for transfers between devices: 37.2 us -> 0 us
  between operations: 14.1 us -> 0.67 us
  Pallas kernels: 38.6 us -> 51.3 us
  starting transfers between devices: 4.46 us -> 0 us
  other arithmetic: 4.44 us -> 0 us
  local copies, waits for them, and re-layouts: 3.58 us -> 6.88 us
    reduce_scatter x1 -> x0, waiting for transfers between devices: 37.2 us -> none  [on_device(): lax.psum_scatter(local, 'ctx', scatter_dimension=0, tiled=True)]
    pallas_call x2, Pallas kernels: 38.6 us -> 51.3 us  [the longest x1 28.1 us: on_device(): pl.pallas_call(functools.partial(exchange_kernel, ctx_count, blocks, chan...]
    convert_element_type x2 -> x0, other arithmetic: 4.44 us -> none  [the longest x1 2.32 us: on_device(): (key[tail].astype(F32) * value[tail].astype(F32)).astype(BF)]
    ppermute x2 -> x0, starting transfers between devices: 4.43 us -> none  [passed_along(): lax.ppermute(value, axis, [(source, source + steps) for source in range(f...]
    unnamed x12 -> x13, local copies, waits for them, and re-layouts: 3.58 us -> 6.88 us
  transfers between devices with their start and end apart: 3 -> 0, of which waited for: 1 -> 0; matrix products, arithmetic and copies ran while one was open for 2% -> 0% of each run, Pallas kernels for 22% -> 0%
where the time goes in v2:
time: 59.1 us; the launch traced here: 58.9 us
  Pallas kernels  51.3 us (87%)
  local copies, waits for them, and re-layouts  6.88 us (12%)
  between operations  0.67 us (1%)
    pallas_call x1, Pallas kernels, on_device(): pl.pallas_call(functools.partial(exchange_kernel, ctx_count, blocks, chan...  28.1 us
    pallas_call x1, Pallas kernels, on_device(): pl.pallas_call(functools.partial(filter_kernel, blocks, chan_group), grid...  23.2 us
    unnamed x13, local copies, waits for them, and re-layouts  6.88 us

profile of v2, /device:TPU:0, one launch (start us, length us, event | category | flops | bytes accessed | tf_op | source)
XLA Modules:
  0.0 58.9 jit_solution(15405459935734360628)
XLA Ops:
  0.6 0.0 copy-start
  0.6 1.4 %copy-done = bf16[384,2048]{1,0:T(8,128)(2,1)S(1)} copy-done((bf16[384,2048]{1,0:T(8,128)(2,1)S(1)}, bf16[384,2048]{1,0:T(8,128)(2,1)}, u32[]{:S(2)}) %copy-start) | copy-done | bytes 1572888
  2.0 0.0 copy-start.1
  2.0 1.4 %copy-done.1 = bf16[384,2048]{1,0:T(8,128)(2,1)S(1)} copy-done((bf16[384,2048]{1,0:T(8,128)(2,1)S(1)}, bf16[384,2048]{1,0:T(8,128)(2,1)}, u32[]{:S(2)}) %copy-start.1) | copy-done | bytes 1572888
  3.5 0.0 copy-start.2
  3.5 1.4 %copy-done.2 = bf16[384,2048]{1,0:T(8,128)(2,1)S(1)} copy-done((bf16[384,2048]{1,0:T(8,128)(2,1)S(1)}, bf16[384,2048]{1,0:T(8,128)(2,1)}, u32[]{:S(2)}) %copy-start.2) | copy-done | bytes 1572888
  4.9 0.0 copy-start.3
  4.9 1.4 %copy-done.3 = bf16[384,2048]{1,0:T(8,128)(2,1)S(1)} copy-done((bf16[384,2048]{1,0:T(8,128)(2,1)S(1)}, bf16[384,2048]{1,0:T(8,128)(2,1)}, u32[]{:S(2)}) %copy-start.3) | copy-done | bytes 1572888
  6.3 0.0 copy-start.5
  6.3 0.7 %copy-done.5 = s32[16]{0:T(128)S(1)} copy-done((s32[16]{0:T(128)S(1)}, s32[16]{0:T(128)}, u32[]{:S(2)}) %copy-start.5) | copy-done | bytes 88
  6.9 0.0 copy-start.4
  6.9 28.1 %exchange.1 = (bf16[128,2048]{1,0:T(8,128)(2,1)S(1)}, bf16[128,2048]{1,0:T(8,128)(2,1)S(1)}, f32[16,128]{1,0:T(8,128)S(1)}) custom-call(s32[16]{0:T(128)S(1)} %copy-done.5, bf16[384,2048]{1,0:T(8,128)(2,1)S(1)} %copy-done, bf16[384,2048]{1,0:T(8,128)(2,1)S(1)} %copy-done.1, bf16[384,2048]{1,0:T(8,128)(2,1)S(1)} %copy-done.2, ...), custom_call_target="tpu_custom_call" | custom-call | tf_op jit(solution)/shard_map/exchange/pallas_call | solution.py:302
  35.1 0.0 copy-done.4
  35.1 23.2 %filter.1 = (bf16[384,2048]{1,0:T(8,128)(2,1)}, bf16[384,2048]{1,0:T(8,128)(2,1)}, bf16[384,2048]{1,0:T(8,128)(2,1)}) custom-call(s32[1]{0:T(128)} %bitcast.base_ref, s32[16]{0:T(128)S(1)} %copy-done.5, bf16[128,128]{1,0:T(8,128)(2,1)S(1)} %copy-done.4, bf16[384,2048]{1,0:T(8,128)(2,1)S(1)} %copy-done, bf16[384,2048]{1,0:T(8,128)(2,1)S(1)} %copy-done.1, ...), custom_call_target="tpu_custom_call" | custom-call | tf_op jit(solution)/shard_map/filter/pallas_call | solution.py:325
  58.3 0.6 %copy.11 = f32[16,128]{1,0:T(8,128)} copy(f32[16,128]{1,0:T(8,128)S(1)} %get-tuple-element.23) | data formatting | bytes 16384
Async XLA Ops:
  0.6 1.4 %copy-start = (bf16[384,2048]{1,0:T(8,128)(2,1)S(1)}, bf16[384,2048]{1,0:T(8,128)(2,1)}, u32[]{:S(2)}) copy-start(bf16[384,2048]{1,0:T(8,128)(2,1)} %gate_ref.3) | copy-start | bytes 4718596
  2.0 1.4 %copy-start.1 = (bf16[384,2048]{1,0:T(8,128)(2,1)S(1)}, bf16[384,2048]{1,0:T(8,128)(2,1)}, u32[]{:S(2)}) copy-start(bf16[384,2048]{1,0:T(8,128)(2,1)} %key_ref.3) | copy-start | bytes 4718596
  3.5 1.4 %copy-start.2 = (bf16[384,2048]{1,0:T(8,128)(2,1)S(1)}, bf16[384,2048]{1,0:T(8,128)(2,1)}, u32[]{:S(2)}) copy-start(bf16[384,2048]{1,0:T(8,128)(2,1)} %value_ref.3) | copy-start | bytes 4718596
  4.9 1.4 %copy-start.3 = (bf16[384,2048]{1,0:T(8,128)(2,1)S(1)}, bf16[384,2048]{1,0:T(8,128)(2,1)}, u32[]{:S(2)}) copy-start(bf16[384,2048]{1,0:T(8,128)(2,1)} %cot_ref.3) | copy-start | bytes 4718596
  6.3 0.7 %copy-start.5 = (s32[16]{0:T(128)S(1)}, s32[16]{0:T(128)}, u32[]{:S(2)}) copy-start(s32[16]{0:T(128)} %lengths_ref.3) | copy-start | bytes 196
  6.9 28.1 %copy-start.4 = (bf16[128,128]{1,0:T(8,128)(2,1)S(1)}, bf16[128,128]{1,0:T(8,128)(2,1)}, u32[]{:S(2)}) copy-start(bf16[128,128]{1,0:T(8,128)(2,1)} %filters_ref.1) | copy-start | bytes 98308

commit v3 on v2

--- a/solution.py
+++ b/solution.py
@@ -11,6 +11,8 @@
 BF = jnp.bfloat16
 F32 = jnp.float32
 CHUNK = 128
+PAIR = 2
+GRANT = 62 * 2**20
 
 
 def doc_ids(lengths_ref, first, shape, dim):
@@ -78,6 +80,9 @@
 def correlate(cots, windows, masks, chan_group):
     taps = CHUNK
     lane = lax.broadcasted_iota(jnp.int32, (1, taps), 1)
+    before = lax.broadcasted_iota(jnp.int32, (taps, taps), 1) > lax.broadcasted_iota(
+        jnp.int32, (taps, taps), 0
+    )
     per = taps // chan_group
     totals = [None] * per
     picks = [
@@ -90,8 +95,8 @@
             stacked, window, (((1,), (1,)), ((), ())), preferred_element_type=F32
         )
         for f in range(per):
-            got = every[f * taps : (f + 1) * taps] * mask[...]
-            got = got[:, :taps] + got[:, taps:]
+            got = every[f * taps : (f + 1) * taps]
+            got = jnp.where(before, got[:, :taps], got[:, taps:]) * mask[...]
             totals[f] = got if totals[f] is None else totals[f] + got
     sums = []
     for total in totals:
@@ -125,7 +130,7 @@
 ):
     taps = CHUNK
     step = pl.program_id(0)
-    steps = pl.num_programs(0) // 2
+    steps = pl.num_programs(0) - 1
     per = CHUNK // chan_group
     me = lax.axis_index("ctx")
     share = taps // n
@@ -174,7 +179,8 @@
 
         for i in range(blocks):
             first = (me * blocks + i) * taps
-            mask_c[i, :, :taps], mask_c[i, :, taps:] = band_masks(lengths_ref, first, True)
+            lower, upper = band_masks(lengths_ref, first, True)
+            mask_c[i] = lower + upper
 
     @pl.when(step < steps)
     def _():
@@ -182,13 +188,16 @@
         filt_cot = (
             cot_ref[taps:].astype(F32) * gate_ref[taps:].astype(F32)
         ).astype(BF)
-        tops[step] = product[:taps]
         inner = range(1, blocks)
-        cots = [filt_cot[(i - 1) * taps : i * taps] for i in inner]
-        windows = [product[(i - 1) * taps : (i + 1) * taps] for i in inner]
-        sums = correlate(cots, windows, [mask_c.at[i] for i in inner], chan_group)
-        for f in range(per):
-            corr_ref[step * per + f] = sums[f]
+        for p in range(PAIR):
+            lanes = slice(p * CHUNK, (p + 1) * CHUNK)
+            g = step * PAIR + p
+            tops[g] = product[:taps, lanes]
+            cots = [filt_cot[(i - 1) * taps : i * taps, lanes] for i in inner]
+            windows = [product[(i - 1) * taps : (i + 1) * taps, lanes] for i in inner]
+            sums = correlate(cots, windows, [mask_c.at[i] for i in inner], chan_group)
+            for f in range(per):
+                corr_ref[g * per + f] = sums[f]
 
     @pl.when(step == steps)
     def _():
@@ -205,17 +214,15 @@
         prev_ref[...] = got_p[...]
         later_ref[...] = got_c[...]
 
-    @pl.when(step >= steps)
-    def _():
-        g = step - steps
-        lanes = pl.ds(pl.multiple_of(g * CHUNK, CHUNK), CHUNK)
-        window = jnp.concatenate([got_p[:, lanes], tops[g]], axis=0)
-        sums = correlate([send_c[:, lanes]], [window], [mask_c.at[0]], chan_group)
-        for f in range(per):
-            corr_ref[g * per + f] = corr_ref[g * per + f] + sums[f]
-
-    @pl.when(step == 2 * steps - 1)
-    def _():
+        def edge(g, carry):
+            lanes = pl.ds(pl.multiple_of(g * CHUNK, CHUNK), CHUNK)
+            window = jnp.concatenate([got_p[:, lanes], tops[g]], axis=0)
+            sums = correlate([send_c[:, lanes]], [window], [mask_c.at[0]], chan_group)
+            for f in range(per):
+                corr_ref[g * per + f] = corr_ref[g * per + f] + sums[f]
+            return carry
+
+        lax.fori_loop(0, steps * PAIR, edge, 0, unroll=2)
         local = collapse(corr_ref, scale)
         for i in range(n):
             local_ref[i] = local[i * share : (i + 1) * share]
@@ -258,25 +265,27 @@
                 mask[i, :, taps:] = right.astype(BF)
 
     per = CHUNK // chan_group
-    here = pl.ds(pl.multiple_of(pl.program_id(0) * per, per), per)
-    key = key_ref[...].astype(F32)
-    value = value_ref[...].astype(F32)
-    cot = cot_ref[...].astype(F32)
-    product = jnp.concatenate([prev_ref[...], (key * value).astype(BF)], axis=0)
-    filt_cot = jnp.concatenate(
-        [(cot * gate_ref[...].astype(F32)).astype(BF), later_ref[...]], axis=0
-    )
-    windows = [product[i * taps : (i + 2) * taps] for i in range(blocks)]
-    outs = convolve(taps_f[here], mask_f, lhs_f, windows, chan_group)
-    for i, out in enumerate(outs):
-        rows = slice(i * taps, (i + 1) * taps)
-        gg_ref[rows] = (cot[rows] * out).astype(BF)
-    ahead = [filt_cot[i * taps : (i + 2) * taps] for i in range(blocks)]
-    outs = convolve(taps_b[here], mask_b, lhs_b, ahead, chan_group)
-    for i, out in enumerate(outs):
-        rows = slice(i * taps, (i + 1) * taps)
-        kg_ref[rows] = (out * value[rows]).astype(BF)
-        vg_ref[rows] = (out * key[rows]).astype(BF)
+    for p in range(PAIR):
+        lanes = slice(p * CHUNK, (p + 1) * CHUNK)
+        here = pl.ds(pl.multiple_of((pl.program_id(0) * PAIR + p) * per, per), per)
+        key = key_ref[:, lanes].astype(F32)
+        value = value_ref[:, lanes].astype(F32)
+        cot = cot_ref[:, lanes].astype(F32)
+        product = jnp.concatenate([prev_ref[:, lanes], (key * value).astype(BF)], axis=0)
+        filt_cot = jnp.concatenate(
+            [(cot * gate_ref[:, lanes].astype(F32)).astype(BF), later_ref[:, lanes]], axis=0
+        )
+        windows = [product[i * taps : (i + 2) * taps] for i in range(blocks)]
+        outs = convolve(taps_f[here], mask_f, lhs_f.at[p], windows, chan_group)
+        for i, out in enumerate(outs):
+            rows = slice(i * taps, (i + 1) * taps)
+            gg_ref[rows, lanes] = (cot[rows] * out).astype(BF)
+        ahead = [filt_cot[i * taps : (i + 2) * taps] for i in range(blocks)]
+        outs = convolve(taps_b[here], mask_b, lhs_b.at[p], ahead, chan_group)
+        for i, out in enumerate(outs):
+            rows = slice(i * taps, (i + 1) * taps)
+            kg_ref[rows, lanes] = (out * value[rows]).astype(BF)
+            vg_ref[rows, lanes] = (out * key[rows]).astype(BF)
 
 
 def on_device(gate, key, value, filters, lengths, cotangent):
@@ -288,27 +297,27 @@
     share = taps // ctx_count
     base = (lax.axis_index("ctx") * row_count).astype(jnp.int32).reshape(1)
     scale = 1.0 / math.sqrt(row_count * ctx_count)
-    steps = width // CHUNK
+    steps = width // (PAIR * CHUNK)
     per = CHUNK // chan_group
     smem = pl.BlockSpec(memory_space=pltpu.SMEM)
-    strip = pl.BlockSpec((row_count, CHUNK), lambda g: (0, g))
-    once = pl.BlockSpec((row_count, CHUNK), lambda g: (0, jnp.minimum(g, steps - 1)))
+    strip = pl.BlockSpec((row_count, PAIR * CHUNK), lambda g: (0, g))
+    once = pl.BlockSpec((row_count, PAIR * CHUNK), lambda g: (0, jnp.minimum(g, steps - 1)))
     head = pl.BlockSpec((taps, width), lambda g: (0, 0))
     bottom = pl.BlockSpec((taps, width), lambda g: (blocks - 1, 0))
-    top = pl.BlockSpec((taps, CHUNK), lambda g: (0, g))
+    top = pl.BlockSpec((taps, PAIR * CHUNK), lambda g: (0, g))
     full = jax.ShapeDtypeStruct((row_count, width), BF)
     edge = jax.ShapeDtypeStruct((taps, width), BF)
     wide = pltpu.VMEM((taps, width), BF)
     prev, later, filter_grad = pl.pallas_call(
         functools.partial(exchange_kernel, ctx_count, blocks, chan_group, scale),
-        grid=(2 * steps,),
+        grid=(steps + 1,),
         in_specs=[smem, once, once, once, once, bottom, bottom, head, head],
         out_specs=[head, head, pl.BlockSpec((share, filt_count), lambda g: (0, 0))],
         out_shape=[edge, edge, jax.ShapeDtypeStruct((share, filt_count), F32)],
         scratch_shapes=[
             wide, wide, wide, wide,
-            pltpu.VMEM((steps, taps, CHUNK), BF),
-            pltpu.VMEM((blocks, taps, 2 * taps), F32),
+            pltpu.VMEM((steps * PAIR, taps, CHUNK), BF),
+            pltpu.VMEM((blocks, taps, taps), F32),
             pltpu.VMEM((filt_count, 8, taps), F32),
             pltpu.VMEM((ctx_count, share, filt_count), F32),
             pltpu.VMEM((ctx_count, share, filt_count), F32),
@@ -318,7 +327,7 @@
             pltpu.SemaphoreType.DMA((ctx_count,)),
         ],
         compiler_params=pltpu.CompilerParams(
-            vmem_limit_bytes=40 * 2**20, collective_id=0, has_side_effects=True
+            vmem_limit_bytes=GRANT, collective_id=0, has_side_effects=True
         ),
         name="exchange",
     )(lengths, gate, key, value, cotangent, key, value, gate, cotangent)
@@ -336,10 +345,10 @@
             pltpu.VMEM((filt_count, taps), F32),
             pltpu.VMEM((blocks, taps, 2 * taps), BF),
             pltpu.VMEM((blocks, taps, 2 * taps), BF),
-            pltpu.VMEM((blocks, per * taps, 2 * taps), BF),
-            pltpu.VMEM((blocks, per * taps, 2 * taps), BF),
+            pltpu.VMEM((PAIR, blocks, per * taps, 2 * taps), BF),
+            pltpu.VMEM((PAIR, blocks, per * taps, 2 * taps), BF),
         ],
-        compiler_params=pltpu.CompilerParams(vmem_limit_bytes=40 * 2**20),
+        compiler_params=pltpu.CompilerParams(vmem_limit_bytes=GRANT),
         name="filter",
     )(base, lengths, filters, gate, key, value, cotangent, prev, later)
     return (gate_grad, key_grad, value_grad, filter_grad)

time: 59.1 us -> 49 us (0.83)
  local copies, waits for them, and re-layouts: 6.88 us -> 0.61 us
  Pallas kernels: 51.3 us -> 47.5 us
    unnamed x13 -> x3, local copies, waits for them, and re-layouts: 6.88 us -> 0.61 us
    pallas_call x1, Pallas kernels: 23.2 us -> 20 us  [on_device(): pl.pallas_call(functools.partial(filter_kernel, blocks, chan_group), grid...]
    pallas_call x1, Pallas kernels: 28.1 us -> 27.4 us  [on_device(): pl.pallas_call(functools.partial(exchange_kernel, ctx_count, blocks, chan...]
where the time goes in v3:
time: 49 us; the launch traced here: 48.7 us
  Pallas kernels  47.5 us (97%)
  between operations  0.66 us (1%)
  local copies, waits for them, and re-layouts  0.61 us (1%)
    pallas_call x1, Pallas kernels, on_device(): pl.pallas_call(functools.partial(exchange_kernel, ctx_count, blocks, chan...  27.4 us
    pallas_call x1, Pallas kernels, on_device(): pl.pallas_call(functools.partial(filter_kernel, blocks, chan_group), grid...  20 us

profile of v3, /device:TPU:0, one launch (start us, length us, event | category | flops | bytes accessed | tf_op | source)
XLA Modules:
  0.0 48.7 jit_solution(6328857951245173200)
XLA Ops:
  0.6 27.4 %exchange.1 = (bf16[128,2048]{1,0:T(8,128)(2,1)}, bf16[128,2048]{1,0:T(8,128)(2,1)}, f32[16,128]{1,0:T(8,128)}) custom-call(s32[16]{0:T(128)} %lengths_ref.3, bf16[384,2048]{1,0:T(8,128)(2,1)} %gate_ref.3, bf16[384,2048]{1,0:T(8,128)(2,1)} %key_ref.3, bf16[384,2048]{1,0:T(8,128)(2,1)} %value_ref.3, bf16[384,2048]{1,0:T(8,128)(2,1)} %cot_ref.3, ...), custom_call_target="tpu_custom_call" | custom-call | tf_op jit(solution)/shard_map/exchange/pallas_call | solution.py:311
  28.1 0.0 copy-start
  28.1 20.0 %filter.1 = (bf16[384,2048]{1,0:T(8,128)(2,1)}, bf16[384,2048]{1,0:T(8,128)(2,1)}, bf16[384,2048]{1,0:T(8,128)(2,1)}) custom-call(s32[1]{0:T(128)} %bitcast.base_ref, s32[16]{0:T(128)} %lengths_ref.3, bf16[128,128]{1,0:T(8,128)(2,1)} %filters_ref.1, bf16[384,2048]{1,0:T(8,128)(2,1)} %gate_ref.3, bf16[384,2048]{1,0:T(8,128)(2,1)} %key_ref.3, ...), custom_call_target="tpu_custom_call" | custom-call | tf_op jit(solution)/shard_map/filter/pallas_call | solution.py:334
  48.1 0.0 copy-done
  48.1 0.6 %copy.11 = f32[16,128]{1,0:T(8,128)} copy(f32[16,128]{1,0:T(8,128)S(1)} %copy-done) | data formatting | bytes 16384
Async XLA Ops:
  28.1 20.0 %copy-start = (f32[16,128]{1,0:T(8,128)S(1)}, f32[16,128]{1,0:T(8,128)}, u32[]{:S(2)}) copy-start(f32[16,128]{1,0:T(8,128)} %get-tuple-element.23) | copy-start | bytes 24580

commit v4 on v3

--- a/solution.py
+++ b/solution.py
@@ -57,23 +57,20 @@
     return left, right
 
 
-def convolve(tap_rows, mask_ref, lhs_ref, inputs, chan_group):
+def convolve(tap_rows, mask_ref, inputs, chan_group):
     taps = CHUNK
     lane = lax.broadcasted_iota(jnp.int32, (taps, taps), 1)
     per = tap_rows.shape[0]
+    outs = [None] * len(inputs)
     for f in range(per):
         spread = jnp.broadcast_to(tap_rows[f : f + 1], (taps, taps))
         circ = pltpu.roll(spread, 0, 1, stride=1, stride_axis=0).astype(BF)
-        for i in range(len(inputs)):
-            lhs_ref[i, f * taps : (f + 1) * taps, :taps] = circ * mask_ref[i, :, :taps]
-            lhs_ref[i, f * taps : (f + 1) * taps, taps:] = circ * mask_ref[i, :, taps:]
-    outs = []
-    for i, x in enumerate(inputs):
-        got = jnp.dot(lhs_ref[i], x, preferred_element_type=F32)
-        total = got[:taps]
-        for f in range(1, per):
-            total = jnp.where(lane >= f * chan_group, got[f * taps : (f + 1) * taps], total)
-        outs.append(total)
+        for i, x in enumerate(inputs):
+            banded = jnp.concatenate(
+                [circ * mask_ref[i, :, :taps], circ * mask_ref[i, :, taps:]], axis=1
+            )
+            got = jnp.dot(banded, x, preferred_element_type=F32)
+            outs[i] = got if f == 0 else jnp.where(lane >= f * chan_group, got, outs[i])
     return outs
 
 
@@ -89,13 +86,11 @@
         jnp.where((lane >= f * chan_group) & (lane < (f + 1) * chan_group), 1.0, 0.0).astype(BF)
         for f in range(per)
     ]
-    for cot, window, mask in zip(cots, windows, masks):
-        stacked = jnp.concatenate([cot * pick for pick in picks], axis=0)
-        every = lax.dot_general(
-            stacked, window, (((1,), (1,)), ((), ())), preferred_element_type=F32
-        )
-        for f in range(per):
-            got = every[f * taps : (f + 1) * taps]
+    for f in range(per):
+        for cot, window, mask in zip(cots, windows, masks):
+            got = lax.dot_general(
+                cot * picks[f], window, (((1,), (1,)), ((), ())), preferred_element_type=F32
+            )
             got = jnp.where(before, got[:, :taps], got[:, taps:]) * mask[...]
             totals[f] = got if totals[f] is None else totals[f] + got
     sums = []
@@ -250,7 +245,7 @@
 def filter_kernel(
     blocks, chan_group, base_ref, lengths_ref, filters_ref, gate_ref, key_ref, value_ref, cot_ref,
     prev_ref, later_ref,
-    gg_ref, kg_ref, vg_ref, taps_f, taps_b, mask_f, mask_b, lhs_f, lhs_b,
+    gg_ref, kg_ref, vg_ref, taps_f, taps_b, mask_f, mask_b,
 ):
     taps = CHUNK
 
@@ -276,12 +271,12 @@
             [(cot * gate_ref[:, lanes].astype(F32)).astype(BF), later_ref[:, lanes]], axis=0
         )
         windows = [product[i * taps : (i + 2) * taps] for i in range(blocks)]
-        outs = convolve(taps_f[here], mask_f, lhs_f.at[p], windows, chan_group)
+        outs = convolve(taps_f[here], mask_f, windows, chan_group)
         for i, out in enumerate(outs):
             rows = slice(i * taps, (i + 1) * taps)
             gg_ref[rows, lanes] = (cot[rows] * out).astype(BF)
         ahead = [filt_cot[i * taps : (i + 2) * taps] for i in range(blocks)]
-        outs = convolve(taps_b[here], mask_b, lhs_b.at[p], ahead, chan_group)
+        outs = convolve(taps_b[here], mask_b, ahead, chan_group)
         for i, out in enumerate(outs):
             rows = slice(i * taps, (i + 1) * taps)
             kg_ref[rows, lanes] = (out * value[rows]).astype(BF)
@@ -298,7 +293,6 @@
     base = (lax.axis_index("ctx") * row_count).astype(jnp.int32).reshape(1)
     scale = 1.0 / math.sqrt(row_count * ctx_count)
     steps = width // (PAIR * CHUNK)
-    per = CHUNK // chan_group
     smem = pl.BlockSpec(memory_space=pltpu.SMEM)
     strip = pl.BlockSpec((row_count, PAIR * CHUNK), lambda g: (0, g))
     once = pl.BlockSpec((row_count, PAIR * CHUNK), lambda g: (0, jnp.minimum(g, steps - 1)))
@@ -345,8 +339,6 @@
             pltpu.VMEM((filt_count, taps), F32),
             pltpu.VMEM((blocks, taps, 2 * taps), BF),
             pltpu.VMEM((blocks, taps, 2 * taps), BF),
-            pltpu.VMEM((PAIR, blocks, per * taps, 2 * taps), BF),
-            pltpu.VMEM((PAIR, blocks, per * taps, 2 * taps), BF),
         ],
         compiler_params=pltpu.CompilerParams(vmem_limit_bytes=GRANT),
         name="filter",

time: 49 us -> 48.1 us (0.982)
  Pallas kernels: 47.5 us -> 46.6 us
    pallas_call x1, Pallas kernels: 20 us -> 19.1 us  [on_device(): pl.pallas_call(functools.partial(filter_kernel, blocks, chan_group), grid...]
where the time goes in v4:
time: 48.1 us; the launch traced here: 47.9 us
  Pallas kernels  46.6 us (97%)
  between operations  0.66 us (1%)
  local copies, waits for them, and re-layouts  0.61 us (1%)
    pallas_call x1, Pallas kernels, on_device(): pl.pallas_call(functools.partial(exchange_kernel, ctx_count, blocks, chan...  27.5 us
    pallas_call x1, Pallas kernels, on_device(): pl.pallas_call(functools.partial(filter_kernel, blocks, chan_group), grid...  19.1 us

profile of v4, /device:TPU:0, one launch (start us, length us, event | category | flops | bytes accessed | tf_op | source)
XLA Modules:
  0.0 47.9 jit_solution(4360939528080228697)
XLA Ops:
  0.6 27.5 %exchange.1 = (bf16[128,2048]{1,0:T(8,128)(2,1)}, bf16[128,2048]{1,0:T(8,128)(2,1)}, f32[16,128]{1,0:T(8,128)}) custom-call(s32[16]{0:T(128)} %lengths_ref.3, bf16[384,2048]{1,0:T(8,128)(2,1)} %gate_ref.3, bf16[384,2048]{1,0:T(8,128)(2,1)} %key_ref.3, bf16[384,2048]{1,0:T(8,128)(2,1)} %value_ref.3, bf16[384,2048]{1,0:T(8,128)(2,1)} %cot_ref.3, ...), custom_call_target="tpu_custom_call" | custom-call | tf_op jit(solution)/shard_map/exchange/pallas_call | solution.py:305
  28.1 0.0 copy-start
  28.2 19.1 %filter.1 = (bf16[384,2048]{1,0:T(8,128)(2,1)}, bf16[384,2048]{1,0:T(8,128)(2,1)}, bf16[384,2048]{1,0:T(8,128)(2,1)}) custom-call(s32[1]{0:T(128)} %bitcast.base_ref, s32[16]{0:T(128)} %lengths_ref.3, bf16[128,128]{1,0:T(8,128)(2,1)} %filters_ref.1, bf16[384,2048]{1,0:T(8,128)(2,1)} %gate_ref.3, bf16[384,2048]{1,0:T(8,128)(2,1)} %key_ref.3, ...), custom_call_target="tpu_custom_call" | custom-call | tf_op jit(solution)/shard_map/filter/pallas_call | solution.py:328
  47.3 0.0 copy-done
  47.3 0.6 %copy.11 = f32[16,128]{1,0:T(8,128)} copy(f32[16,128]{1,0:T(8,128)S(1)} %copy-done) | data formatting | bytes 16384
Async XLA Ops:
  28.1 19.1 %copy-start = (f32[16,128]{1,0:T(8,128)S(1)}, f32[16,128]{1,0:T(8,128)}, u32[]{:S(2)}) copy-start(f32[16,128]{1,0:T(8,128)} %get-tuple-element.23) | copy-start | bytes 24580
